TPU v7x, 32 devices: a whole 2x2x4 slice. The times are simulated.
32 devices in a mesh: group: 2 (over x), slab: 16 (over z, y, core).
Axes of the slice: x: 2, y: 2, z: 4, core: 2. Of those that a mesh axis runs over, the one named last changes fastest.
Arguments:
- field: float32 [4, 64, 64, 4096], P('group', 'slab'), parts along dimension 0, may hold values from -6 to 6
- out_grad: float32 [4, 64, 64, 4096], P('group', 'slab'), parts along dimension 0, may hold values from -6 to 6
- kept: int32 [48], replicated, may hold values from 0 to 511, as said below
- mixing: float32 [48, 32, 64, 128], P('slab'), may hold values from -3 to 3
Outputs:
- grad_mixing: float32 [96, 32, 64, 128], P(('group', 'slab')), parts along dimension 0
- grad_field: float32 [4, 64, 64, 4096], P('group', 'slab'), parts along dimension 0
There are 2 independent parts, one for each index of `group`. A program takes and returns all parts, laid end to end along the dimension named above; an argument that names none is the same for every part. Nothing has to cross between parts.
Inputs may be any that keep to these rules, and one draw needn't show every extreme that they name: `kept`: 48 distinct pencil indices; pencil 0 and pencil 32 * 16 - 1 are always among them.
All inputs are finite; a program needn't handle non-finite values.
Results may differ from a plain program's by a relative error of at most 0.00011.
Values sent between devices are 32-bit elements; how exact they have to be, the bound alone decides.
A program may use at most 128 MiB of HBM per device.

v0:
```python
import functools
import math

import jax
import jax.numpy as jnp
from jax import lax
from jax.experimental import pallas as pl
from jax.experimental.pallas import tpu as pltpu
from jax.sharding import PartitionSpec as P

NX = 64
NY = 64
NZ = 64
KX = 32
KY = 32
KZ = 16
CELLS = NY * NZ
C = 64
LANES = 2 * C
UNIT = 2.0 * math.pi / 64
SCALE = 1.0 / math.sqrt(NX * NY * NZ)
HIGH = lax.Precision.HIGHEST
F32 = jnp.float32
BF16 = jnp.bfloat16
MESH = pl.DeviceIdType.MESH


def split(v):
    hi = v.astype(BF16)
    return hi, (v - hi.astype(F32)).astype(BF16)


def dot(a, b):
    return jnp.dot(a, b, preferred_element_type=F32)


def iota(shape, dim):
    return lax.broadcasted_iota(jnp.int32, shape, dim)


def freqs(kept):
    ky = lax.div(kept, KZ)
    fy = jnp.where(ky < KY // 2, ky, ky - KY)
    return fy, lax.rem(kept, KZ)


def turns(count):
    return (count & 63).astype(F32) * UNIT


def build_rows(kept, table, rows):
    fy, fz = freqs(kept)
    lane = iota((rows, LANES), 1)
    phase = (iota((rows, LANES), 0) & 1) * 16
    used = (kept >= 0).astype(F32)
    base = turns(fy * (lane >> 6) + fz * (lane & 63) + phase)
    step = turns(2 * fy)
    sc, ss = jnp.cos(step), jnp.sin(step)

    def body(t, carry):
        c, s = carry
        hi, lo = split(c)
        at = pl.ds(pl.multiple_of(t * LANES, LANES), LANES)
        table[pl.ds(0, rows), at] = hi
        table[pl.ds(rows, rows), at] = lo
        return c * sc - s * ss, s * sc + c * ss

    lax.fori_loop(0, CELLS // LANES, body, (jnp.cos(base) * used, jnp.sin(base) * used))


def build_columns(kept, table, rows):
    kept = jnp.broadcast_to(kept, (NZ, rows))
    fy, fz = freqs(kept)
    phase = (iota((NZ, rows), 1) & 1) * 16
    used = (kept >= 0).astype(F32)
    base = turns(fz * iota((NZ, rows), 0) + phase)
    step = turns(fy)
    sc, ss = jnp.cos(step), jnp.sin(step)

    def body(t, carry):
        c, s = carry
        hi, lo = split(c)
        at = pl.ds(pl.multiple_of(t * NZ, NZ), NZ)
        table[at, pl.ds(0, rows)] = hi
        table[at, pl.ds(rows, rows)] = lo
        return c * sc - s * ss, s * sc + c * ss

    lax.fori_loop(0, NY, body, (jnp.cos(base) * used, jnp.sin(base) * used))


def x_of(index, n, planes):
    return lax.rem(index, n) * planes + lax.div(index, n)


def signed_x(a):
    return jnp.where(a < KX // 2, a, a - KX)


def swap(v):
    return pltpu.roll(v, C, 1)


def gelu_slope(v):
    a = jnp.abs(v)
    t = 1.0 / (1.0 + a * (0.3275911 / math.sqrt(2.0)))
    tail = t * (0.127414796 + t * (-0.142248368 + t * (0.7107068705 + t * (-0.7265760135 + t * 0.5307027145))))
    over = 1.0 + jnp.exp(-0.5 * v * v) * (a * (1.0 / math.sqrt(2.0 * math.pi)) - tail)
    return jnp.where(v >= 0, over, 1.0 - over)


def lines_matrix(got, b, store, n, planes, owned):
    for x in range(planes):
        for g in range(2 * owned):
            store[:, g, pl.ds(x * C, C)] = got[b, :, x, pl.ds(g * C, C)]
    lines = store[...].reshape(n * 8, planes * C).T
    hi, lo = split(lines)
    return jnp.concatenate([hi, hi], axis=1), lo


def main_kernel(
    n, planes, owned,
    kept_s, kept_r, kept_c, field, out_grad, mixing,
    modes_out, grads_out, lines_out,
    f_v, o_v, w_v, w_b, t_r, t_c, acc, store, left, res, mid, send, recv,
    f_sem, o_sem, w_sem, send_sem, recv_sem, out_sem,
):
    rows = n * 8
    samples = f_v.shape[0]
    chunks = f_sem.shape[1]
    width = CELLS // chunks
    me = lax.axis_index("slab")
    barrier = pltpu.get_barrier_semaphore()

    def greet(k, _):
        pl.semaphore_signal(barrier, inc=1, device_id={"slab": lax.rem(me + k, n)}, device_id_type=MESH)
        return 0

    lax.fori_loop(1, n, greet, 0)

    def load(src, dst, sem, b, k):
        at = pl.ds(k * width, width)
        return pltpu.make_async_copy(src.at[b, :, :, at], dst.at[b, :, :, at], sem.at[b, k])

    w_load = pltpu.make_async_copy(mixing, w_v, w_sem)
    for b in range(samples):
        for k in range(chunks):
            load(field, f_v, f_sem, b, k).start()
    w_load.start()
    for b in range(samples):
        for k in range(chunks):
            load(out_grad, o_v, o_sem, b, k).start()

    build_columns(kept_c[0:1, :], t_c, rows)

    turn = signed_x(iota((KX, NX), 0)) * x_of(iota((KX, NX), 1), n, planes)
    to_modes = jnp.concatenate([jnp.cos(turns(turn)), jnp.sin(turns(turn))], axis=0)
    turn = signed_x(iota((NX, KX), 1)) * x_of(iota((NX, KX), 0), n, planes)
    to_lines = jnp.concatenate([jnp.cos(turns(turn)), jnp.sin(turns(turn))], axis=0)
    sign = jnp.where(iota((KX, LANES), 1) < C, 1.0, -1.0).astype(F32)
    sign_x = jnp.where(iota((NX, LANES), 1) < C, -1.0, 1.0).astype(F32)

    def factor(j):
        kept = kept_s[me * owned + j]
        return jnp.where(lax.rem(kept, KZ) > 0, 2.0, 1.0).astype(F32) * SCALE

    factors = [factor(j) for j in range(owned)]

    def exchange(phase, b):
        def go(k, _):
            to = lax.rem(me + k, n)
            pltpu.make_async_remote_copy(
                src_ref=send.at[phase, b, to],
                dst_ref=recv.at[phase, b, me],
                send_sem=send_sem.at[phase, b],
                recv_sem=recv_sem.at[phase, b],
                device_id={"slab": to},
                device_id_type=MESH,
            ).start()
            return 0

        lax.fori_loop(1, n, go, 0)
        recv[phase, b, me] = send[phase, b, me]

    def arrive(phase, b):
        part = recv.at[phase, b, pl.ds(0, n - 1)]
        pltpu.make_async_copy(part, part, recv_sem.at[phase, b]).wait()

    def spread(phase, b):
        store[...] = acc[...].T.reshape(n, 8, planes * C)
        for x in range(planes):
            pieces = [store[:, g, pl.ds(x * C, C)] for g in range(2 * owned)]
            send[phase, b, :, x, :] = jnp.concatenate(pieces, axis=1)

    def plane_products(v, at):
        hi, lo = split(v)
        first = dot(hi, t_c[at, :])
        return first[:, :rows] + first[:, rows:] + dot(lo, t_c[at, pl.ds(0, rows)])

    def forward_field(b):
        for k in range(chunks):
            load(field, f_v, f_sem, b, k).wait()
            v = f_v[b, :, :, pl.ds(k * width, width)].reshape(planes * C, width)
            got = plane_products(v, pl.ds(k * width, width))
            acc[...] = got if k == 0 else acc[...] + got

    def received_modes(phase, b):
        lines = jnp.concatenate([recv[phase, b, :, x, :] for x in range(planes)], axis=0)
        both = jnp.dot(to_modes, lines, preferred_element_type=F32, precision=HIGH)
        out = []
        for j in range(owned):
            at = slice(j * LANES, (j + 1) * LANES)
            out.append(both[:KX, at] + swap(both[KX:, at]) * sign)
        return out

    def products(transposed):
        dims = (((1,), (1 if transposed else 0,)), ((), ()))

        def body(i, _):
            for u in range(8):
                at = i * 8 + u
                res[at] = lax.dot_general(left[at].astype(BF16), w_b[at], dims, preferred_element_type=F32)
            return 0

        lax.fori_loop(0, owned * KX // 8, body, 0)

    def send_lines(phase, b, modes):
        modes = jnp.concatenate(modes, axis=1)
        both = jnp.dot(to_lines, modes, preferred_element_type=F32, precision=HIGH)
        out = []
        for j in range(owned):
            at = slice(j * LANES, (j + 1) * LANES)
            out.append(both[:NX, at] + swap(both[NX:, at]) * sign_x)
        lines = jnp.concatenate(out, axis=1)
        for x in range(planes):
            send[phase, b, :, x, :] = lines[x * n : (x + 1) * n, :]
        exchange(phase, b)

    low = iota((KX, LANES), 1) < C

    def mix(b):
        for j, modes in enumerate(received_modes(0, b)):
            modes = modes * SCALE
            mid[0, j, b] = modes
            hi = modes.astype(BF16).astype(F32)
            lo = (modes - hi).astype(BF16).astype(F32)
            at = pl.ds(j * KX, KX)
            left[at, 0, :] = jnp.where(low, hi, swap(hi))
            left[at, 1, :] = jnp.where(low, swap(hi), hi)
            left[at, 2, :] = jnp.where(low, lo, 0.0)
            left[at, 3, :] = jnp.where(low, swap(lo), 0.0)
        products(False)
        out = []
        for j in range(owned):
            at = pl.ds(j * KX, KX)
            first = res[at, 0, :] + res[at, 2, :]
            second = res[at, 1, :] + res[at, 3, :]
            out.append((first - swap(second) * sign) * factors[j])
        send_lines(1, b, out)

    def unmix(b):
        for j, grads in enumerate(received_modes(2, b)):
            grads = grads * factors[j]
            mid[1, j, b] = grads
            hi = grads.astype(BF16).astype(F32)
            lo = (grads - hi).astype(BF16).astype(F32)
            at = pl.ds(j * KX, KX)
            left[at, 0, :] = hi
            left[at, 1, :] = swap(hi) * sign
            left[at, 2, :] = lo
            left[at, 3, :] = swap(lo) * sign
        products(True)
        out = []
        for j in range(owned):
            at = pl.ds(j * KX, KX)
            real_hi, imag_hi = res[at, 0, :], res[at, 1, :]
            real = real_hi + swap(real_hi) + res[at, 2, :]
            imag = imag_hi + swap(imag_hi) + res[at, 3, :]
            out.append(jnp.where(low, real, swap(imag)) * SCALE)
        send_lines(3, b, out)

    def through_cells(b):
        first, second = lines_matrix(recv.at[1], b, store, n, planes, owned)
        for k in range(chunks):
            load(out_grad, o_v, o_sem, b, k).wait()
        acc[...] = jnp.zeros_like(acc)
        step = 256

        def body(k, _):
            at = pl.ds(pl.multiple_of(k * step, step), step)
            pre = dot(first, t_r[:, at]) + dot(second, t_r[pl.ds(0, rows), at])
            v = o_v[b, :, :, at].reshape(planes * C, step) * gelu_slope(pre)
            acc[...] += plane_products(v, at)
            return 0

        lax.fori_loop(0, CELLS // step, body, 0)

    forward_field(0)
    spread(0, 0)
    pl.semaphore_wait(barrier, n - 1)
    exchange(0, 0)
    for b in range(1, samples):
        forward_field(b)
        spread(0, b)
        exchange(0, b)

    build_rows(kept_r[...], t_r, rows)
    left[...] = jnp.zeros_like(left)
    w_load.wait()

    def cut(i, _):
        hi, lo = split(w_v[i])
        w_b[i, pl.ds(0, C), :] = hi
        w_b[i, pl.ds(C, C), :] = lo
        return 0

    lax.fori_loop(0, owned * KX, cut, 0)

    for b in range(samples):
        arrive(0, b)
        mix(b)
    store[...] = jnp.zeros_like(store)
    for b in range(samples):
        arrive(1, b)
        through_cells(b)
        spread(2, b)
        exchange(2, b)
    for b in range(samples):
        arrive(2, b)
        unmix(b)
    outs = [
        pltpu.make_async_copy(mid.at[0], modes_out, out_sem.at[0]),
        pltpu.make_async_copy(mid.at[1], grads_out, out_sem.at[1]),
    ]
    for copy in outs:
        copy.start()
    for b in range(samples):
        arrive(3, b)
    outs.append(pltpu.make_async_copy(recv.at[3], lines_out, out_sem.at[2]))
    outs[2].start()
    for copy in outs:
        copy.wait()
    for phase in range(4):
        for b in range(samples):
            part = send.at[phase, b, pl.ds(0, n - 1)]
            pltpu.make_async_copy(part, part, send_sem.at[phase, b]).wait()


def last_kernel(
    n, planes, owned,
    kept_r, modes, grads, lines,
    gm_out, gf_out,
    t_r, store, lhs, rhs, gm, gf, gm_sem, gf_sem,
):
    rows = n * 8
    samples = gf.shape[0]
    low = iota((KX, LANES), 1) < C
    sign = jnp.where(low, 1.0, -1.0).astype(F32)
    lhs[...] = jnp.zeros_like(lhs)
    rhs[...] = jnp.zeros_like(rhs)
    chunk = KX // 2
    gm_copies = []
    for j in range(owned):
        base = j * KX
        at = pl.ds(base, KX)
        for b in range(samples):
            u, g = modes[j, b], grads[j, b]
            for k, (uu, gg) in enumerate(((u, g), (swap(u), swap(g) * sign))):
                u_hi = uu.astype(BF16).astype(F32)
                u_lo = (uu - u_hi).astype(BF16).astype(F32)
                g_hi = gg.astype(BF16).astype(F32)
                g_lo = (gg - g_hi).astype(BF16).astype(F32)
                row = (b * 2 + k) * 3
                for r, (left, right) in enumerate(((u_hi, g_hi), (u_hi, g_lo), (u_lo, g_hi))):
                    lhs[at, row + r, :] = left
                    rhs[at, row + r, :] = right
    for j in range(owned):
        base = j * KX

        def body(i, _):
            for u in range(4):
                a = base + i * 4 + u
                got = lax.dot_general(
                    lhs[a].astype(BF16), rhs[a].astype(BF16), (((0,), (0,)), ((), ())), preferred_element_type=F32
                )
                gm[a] = got[:C, :]
            return 0

        lax.fori_loop(0, KX // 4, body, 0)
        copy = pltpu.make_async_copy(gm.at[pl.ds(base, KX)], gm_out.at[pl.ds(base, KX)], gm_sem.at[j])
        copy.start()
        gm_copies.append(copy)

    build_rows(kept_r[...], t_r, rows)
    store[...] = jnp.zeros_like(store)
    chunks = gf_sem.shape[1]
    width = CELLS // chunks
    for b in range(samples):
        first, second = lines_matrix(lines, b, store, n, planes, owned)

        def chunk_of(k, b=b):
            at = pl.ds(pl.multiple_of(k * width, width), width)
            return at, pltpu.make_async_copy(gf.at[b, :, :, at], gf_out.at[b, :, :, at], gf_sem.at[b, k])

        def body(k, _):
            at, copy = chunk_of(k)
            out = dot(first, t_r[:, at]) + dot(second, t_r[pl.ds(0, rows), at])
            gf[b, :, :, at] = out.reshape(planes, C, width)
            copy.start()
            return 0

        lax.fori_loop(0, chunks, body, 0)
    for copy in gm_copies:
        copy.wait()
    for b in range(samples):
        def done(k, _, b=b):
            at = pl.ds(pl.multiple_of(k * width, width), width)
            pltpu.make_async_copy(gf.at[b, :, :, at], gf_out.at[b, :, :, at], gf_sem.at[b, k]).wait()
            return 0

        lax.fori_loop(0, chunks, done, 0)


def on_device(n, field, out_grad, kept, mixing):
    samples, planes = field.shape[:2]
    owned = mixing.shape[0]
    rows = n * 8
    kept = kept.astype(jnp.int32)
    each = jnp.broadcast_to(kept.reshape(n, owned, 1), (n, owned, 2)).reshape(n, 2 * owned)
    each = jnp.pad(each, ((0, 0), (0, 8 - 2 * owned)), constant_values=-1).reshape(rows)
    kept_r = jnp.broadcast_to(each[:, None], (rows, LANES))
    kept_c = jnp.broadcast_to(each[None, :], (8, rows))
    vmem = pl.BlockSpec(memory_space=pltpu.VMEM)
    hbm = pl.BlockSpec(memory_space=pl.ANY)
    smem = pl.BlockSpec(memory_space=pltpu.SMEM)
    chunks = 8
    block = (n, planes, owned * LANES)
    modes, grads, lines = pl.pallas_call(
        functools.partial(main_kernel, n, planes, owned),
        out_shape=[
            jax.ShapeDtypeStruct((owned, samples, KX, LANES), F32),
            jax.ShapeDtypeStruct((owned, samples, KX, LANES), F32),
            jax.ShapeDtypeStruct((samples,) + block, F32),
        ],
        in_specs=[smem, vmem, vmem, hbm, hbm, hbm],
        out_specs=[hbm, hbm, hbm],
        scratch_shapes=[
            pltpu.VMEM(field.shape, F32),
            pltpu.VMEM(field.shape, F32),
            pltpu.VMEM((owned * KX, C, LANES), F32),
            pltpu.VMEM((owned * KX, LANES, LANES), BF16),
            pltpu.VMEM((2 * rows, CELLS), BF16),
            pltpu.VMEM((CELLS, 2 * rows), BF16),
            pltpu.VMEM((planes * C, rows), F32),
            pltpu.VMEM((n, 8, planes * C), F32),
            pltpu.VMEM((owned * KX, 8, LANES), F32),
            pltpu.VMEM((owned * KX, 8, LANES), F32),
            pltpu.VMEM((2, owned, samples, KX, LANES), F32),
            pltpu.VMEM((4, samples) + block, F32),
            pltpu.VMEM((4, samples) + block, F32),
            pltpu.SemaphoreType.DMA((samples, chunks)),
            pltpu.SemaphoreType.DMA((samples, chunks)),
            pltpu.SemaphoreType.DMA,
            pltpu.SemaphoreType.DMA((4, samples)),
            pltpu.SemaphoreType.DMA((4, samples)),
            pltpu.SemaphoreType.DMA((3,)),
        ],
        compiler_params=pltpu.CompilerParams(
            collective_id=0, has_side_effects=True, vmem_limit_bytes=56 * 2**20
        ),
    )(kept, kept_r, kept_c, field, out_grad, mixing.reshape(owned * KX, C, LANES))
    grad_mixing, grad_field = pl.pallas_call(
        functools.partial(last_kernel, n, planes, owned),
        out_shape=[
            jax.ShapeDtypeStruct((owned * KX, C, LANES), F32),
            jax.ShapeDtypeStruct(field.shape, F32),
        ],
        in_specs=[vmem, vmem, vmem, vmem],
        out_specs=[hbm, hbm],
        scratch_shapes=[
            pltpu.VMEM((2 * rows, CELLS), BF16),
            pltpu.VMEM((n, 8, planes * C), F32),
            pltpu.VMEM((owned * KX, 16, LANES), F32),
            pltpu.VMEM((owned * KX, 16, LANES), F32),
            pltpu.VMEM((owned * KX, C, LANES), F32),
            pltpu.VMEM(field.shape, F32),
            pltpu.SemaphoreType.DMA((owned,)),
            pltpu.SemaphoreType.DMA((samples, chunks)),
        ],
        compiler_params=pltpu.CompilerParams(vmem_limit_bytes=56 * 2**20),
    )(kept_r, modes, grads, lines)
    return grad_mixing.reshape(mixing.shape), grad_field


def solution(mesh):
    n = mesh.shape["slab"]
    placed = (
        P("group", "slab", None, None),
        P("group", "slab", None, None),
        P(),
        P("slab", None, None, None),
    )
    return jax.shard_map(
        functools.partial(on_device, n),
        mesh=mesh,
        in_specs=placed,
        out_specs=(P(("group", "slab"), None, None, None), P("group", "slab", None, None)),
        check_vma=False,
    )
```

profile of v0, /device:TPU:0, one launch (start us, length us, event | category | flops | bytes accessed | tf_op | source)
XLA Modules:
  0.0 74.4 jit_solution(5262146328086525941)
XLA Ops:
  0.6 0.7 broadcast_in_dim.19
  1.4 0.1 copy.8
  1.5 0.1 copy.10
  1.6 0.1 broadcast_in_dim.21
  1.7 0.6 broadcast_in_dim.23.kept_c
  2.3 0.7 broadcast_in_dim.22.kept_r
  3.0 56.5 %shard_map.59 = (f32[3,2,32,128]{3,2,1,0:T(8,128)}, f32[3,2,32,128]{3,2,1,0:T(8,128)}, f32[2,16,4,384]{3,2,1,0:T(4,128)}) custom-call(s32[48]{0:T(128)} %kept_s.1, s32[128,128]{1,0:T(8,128)} %broadcast_in_dim.22.kept_r, s32[8,128]{1,0:T(8,128)} %broadcast_in_dim.23.kept_c, f32[2,4,64,4096]{3,2,1,0:T(8,128)} %field.1, f32[2,4,64,4096]{3,2,1,0:T(8,128)} %out_grad.1, ...), custom_call_target="tpu_custom_call" | custom-call | tf_op jit(solution)/shard_map/pallas_call | solution.py:437
  59.5 14.9 %shard_map.60 = (f32[96,64,128]{2,1,0:T(8,128)}, f32[2,4,64,4096]{3,2,1,0:T(8,128)}) custom-call(s32[128,128]{1,0:T(8,128)} %broadcast_in_dim.22.kept_r, f32[3,2,32,128]{3,2,1,0:T(8,128)} %get-tuple-element.7.modes, f32[3,2,32,128]{3,2,1,0:T(8,128)} %get-tuple-element.8.grads, f32[2,16,4,384]{3,2,1,0:T(4,128)} %get-tuple-element.9.lines), custom_call_target="tpu_custom_call" | custom-call | tf_op jit(solution)/shard_map/pallas_call | solution.py:471
  (3 shorter events, 0.0 us)
where the time goes:
time: 74.6 us; the launch traced here: 74.4 us
  Pallas kernels  71.4 us (96%)
  local copies, waits for them, and re-layouts  2.33 us (3%)
    pallas_call x1, Pallas kernels, on_device(): pl.pallas_call(functools.partial(main_kernel, n, planes, owned), out_shap...  56.5 us
    pallas_call x1, Pallas kernels, on_device(): pl.pallas_call(functools.partial(last_kernel, n, planes, owned), out_shap...  14.9 us

commit v1 on v0

--- a/solution.py
+++ b/solution.py
@@ -63,6 +63,7 @@
         at = pl.ds(pl.multiple_of(t * LANES, LANES), LANES)
         table[pl.ds(0, rows), at] = hi
         table[pl.ds(rows, rows), at] = lo
+        table[pl.ds(2 * rows, rows), at] = hi
         return c * sc - s * ss, s * sc + c * ss
 
     lax.fori_loop(0, CELLS // LANES, body, (jnp.cos(base) * used, jnp.sin(base) * used))
@@ -102,10 +103,27 @@
 
 def gelu_slope(v):
     a = jnp.abs(v)
-    t = 1.0 / (1.0 + a * (0.3275911 / math.sqrt(2.0)))
+    d = 1.0 + a * (0.3275911 / math.sqrt(2.0))
+    t = pl.reciprocal(d, approx=True)
+    t = t * (2.0 - d * t)
     tail = t * (0.127414796 + t * (-0.142248368 + t * (0.7107068705 + t * (-0.7265760135 + t * 0.5307027145))))
-    over = 1.0 + jnp.exp(-0.5 * v * v) * (a * (1.0 / math.sqrt(2.0 * math.pi)) - tail)
-    return jnp.where(v >= 0, over, 1.0 - over)
+    over = jnp.exp2(v * v * (-0.5 / math.log(2.0))) * (a * (1.0 / math.sqrt(2.0 * math.pi)) - tail)
+    return jnp.where(v >= 0, 1.0 + over, -over)
+
+
+def build_spread(table, halves):
+    count = table.shape[1]
+    k = iota((2 * KX, count), 0) & (KX - 1)
+    column = iota((2 * KX, count), 1)
+    wanted = column >> 7
+    if halves:
+        wanted = wanted + ((column >> 6) & 1) * (KX // 2)
+    table[...] = jnp.where(k == wanted, 1.0, 0.0).astype(BF16)
+
+
+def turned(v):
+    hi = v.astype(BF16).astype(F32)
+    return jnp.concatenate([hi, v - hi], axis=0).T.astype(BF16)
 
 
 def lines_matrix(got, b, store, n, planes, owned):
@@ -114,14 +132,14 @@
             store[:, g, pl.ds(x * C, C)] = got[b, :, x, pl.ds(g * C, C)]
     lines = store[...].reshape(n * 8, planes * C).T
     hi, lo = split(lines)
-    return jnp.concatenate([hi, hi], axis=1), lo
+    return jnp.concatenate([hi, hi, lo], axis=1)
 
 
 def main_kernel(
     n, planes, owned,
     kept_s, kept_r, kept_c, field, out_grad, mixing,
     modes_out, grads_out, lines_out,
-    f_v, o_v, w_v, w_b, t_r, t_c, acc, store, left, res, mid, send, recv,
+    f_v, o_v, w_v, w_t, t_r, t_c, acc, store, pipe, e_mix, e_unmix, res, mid, send, recv,
     f_sem, o_sem, w_sem, send_sem, recv_sem, out_sem,
 ):
     rows = n * 8
@@ -212,16 +230,14 @@
             out.append(both[:KX, at] + swap(both[KX:, at]) * sign)
         return out
 
-    def products(transposed):
-        dims = (((1,), (1 if transposed else 0,)), ((), ()))
-
-        def body(i, _):
-            for u in range(8):
-                at = i * 8 + u
-                res[at] = lax.dot_general(left[at].astype(BF16), w_b[at], dims, preferred_element_type=F32)
-            return 0
-
-        lax.fori_loop(0, owned * KX // 8, body, 0)
+    def total(at, first):
+        out = res[at, first, :]
+        for r in range(first + 1, first + 8):
+            out = out + res[at, r, :]
+        return out
+
+    def fold(v):
+        return v.reshape(C // 8, 8, LANES).sum(axis=0)
 
     def send_lines(phase, b, modes):
         modes = jnp.concatenate(modes, axis=1)
@@ -235,64 +251,87 @@
             send[phase, b, :, x, :] = lines[x * n : (x + 1) * n, :]
         exchange(phase, b)
 
-    low = iota((KX, LANES), 1) < C
-
     def mix(b):
         for j, modes in enumerate(received_modes(0, b)):
-            modes = modes * SCALE
-            mid[0, j, b] = modes
-            hi = modes.astype(BF16).astype(F32)
-            lo = (modes - hi).astype(BF16).astype(F32)
-            at = pl.ds(j * KX, KX)
-            left[at, 0, :] = jnp.where(low, hi, swap(hi))
-            left[at, 1, :] = jnp.where(low, swap(hi), hi)
-            left[at, 2, :] = jnp.where(low, lo, 0.0)
-            left[at, 3, :] = jnp.where(low, swap(lo), 0.0)
-        products(False)
+            mid[0, j, b] = modes * SCALE
+
+        def body(j, _):
+            lhs = turned(mid[0, j, b])
+            for start in range(0, KX, 4):
+                wide = dot(lhs, e_mix[:, start * LANES : (start + 4) * LANES])
+                for a in range(4):
+                    at = j * KX + start + a
+                    w = w_v[at]
+                    m = wide[:, a * LANES : (a + 1) * LANES]
+                    res[at, 0:8, :] = fold(w * m[:C])
+                    res[at, 8:16, :] = fold(w * m[C:])
+            return 0
+
+        lax.fori_loop(0, owned, body, 0)
         out = []
         for j in range(owned):
             at = pl.ds(j * KX, KX)
-            first = res[at, 0, :] + res[at, 2, :]
-            second = res[at, 1, :] + res[at, 3, :]
-            out.append((first - swap(second) * sign) * factors[j])
+            out.append((total(at, 0) - swap(total(at, 8)) * sign) * factors[j])
         send_lines(1, b, out)
 
     def unmix(b):
         for j, grads in enumerate(received_modes(2, b)):
-            grads = grads * factors[j]
-            mid[1, j, b] = grads
-            hi = grads.astype(BF16).astype(F32)
-            lo = (grads - hi).astype(BF16).astype(F32)
-            at = pl.ds(j * KX, KX)
-            left[at, 0, :] = hi
-            left[at, 1, :] = swap(hi) * sign
-            left[at, 2, :] = lo
-            left[at, 3, :] = swap(lo) * sign
-        products(True)
+            mid[1, j, b] = grads * factors[j]
+        half = KX // 2
+
+        def body(j, _):
+            lhs = turned(mid[1, j, b])
+            for start in range(0, half, 4):
+                wide = dot(lhs, e_unmix[:, start * LANES : (start + 4) * LANES])
+                for a in range(4):
+                    at = j * half + start + a
+                    w_re, w_im = w_t[at, :C, :], w_t[at, C:, :]
+                    g = wide[:, a * LANES : (a + 1) * LANES]
+                    res[at, 0:8, :] = fold(w_re * g[:C] + w_im * g[C:])
+                    res[at, 8:16, :] = fold(w_re * g[C:] - w_im * g[:C])
+            return 0
+
+        lax.fori_loop(0, owned, body, 0)
         out = []
+        low_h = iota((half, LANES), 1) < C
         for j in range(owned):
-            at = pl.ds(j * KX, KX)
-            real_hi, imag_hi = res[at, 0, :], res[at, 1, :]
-            real = real_hi + swap(real_hi) + res[at, 2, :]
-            imag = imag_hi + swap(imag_hi) + res[at, 3, :]
-            out.append(jnp.where(low, real, swap(imag)) * SCALE)
+            at = pl.ds(j * half, half)
+            real, imag = total(at, 0), total(at, 8)
+            early = jnp.where(low_h, real, swap(imag))
+            late = jnp.where(low_h, swap(real), imag)
+            out.append(jnp.concatenate([early, late], axis=0) * SCALE)
         send_lines(3, b, out)
 
     def through_cells(b):
-        first, second = lines_matrix(recv.at[1], b, store, n, planes, owned)
+        first = lines_matrix(recv.at[1], b, store, n, planes, owned)
         for k in range(chunks):
             load(out_grad, o_v, o_sem, b, k).wait()
+        step = pipe.shape[3]
+
+        def add(slot, k):
+            at = pl.ds(pl.multiple_of(k * step, step), step)
+            got = dot(pipe[slot, 0], t_c[at, :])
+            acc[...] += got[:, :rows] + got[:, rows:] + dot(pipe[slot, 1], t_c[at, pl.ds(0, rows)])
+
+        def cells(slot, k):
+            at = pl.ds(pl.multiple_of(k * step, step), step)
+            pre = dot(first, t_r[:, at])
+            v = o_v[b, :, :, at].reshape(planes * C, step) * gelu_slope(pre)
+            hi, lo = split(v)
+            pipe[slot, 0] = hi
+            pipe[slot, 1] = lo
+
+        def body(i, _):
+            add(1, jnp.maximum(2 * i - 1, 0))
+            cells(0, 2 * i)
+            add(0, 2 * i)
+            cells(1, 2 * i + 1)
+            return 0
+
         acc[...] = jnp.zeros_like(acc)
-        step = 256
-
-        def body(k, _):
-            at = pl.ds(pl.multiple_of(k * step, step), step)
-            pre = dot(first, t_r[:, at]) + dot(second, t_r[pl.ds(0, rows), at])
-            v = o_v[b, :, :, at].reshape(planes * C, step) * gelu_slope(pre)
-            acc[...] += plane_products(v, at)
-            return 0
-
-        lax.fori_loop(0, CELLS // step, body, 0)
+        pipe[1] = jnp.zeros(pipe.shape[1:], BF16)
+        lax.fori_loop(0, CELLS // step // 2, body, 0)
+        add(1, CELLS // step - 1)
 
     forward_field(0)
     spread(0, 0)
@@ -304,20 +343,23 @@
         exchange(0, b)
 
     build_rows(kept_r[...], t_r, rows)
-    left[...] = jnp.zeros_like(left)
+    build_spread(e_mix, False)
     w_load.wait()
-
-    def cut(i, _):
-        hi, lo = split(w_v[i])
-        w_b[i, pl.ds(0, C), :] = hi
-        w_b[i, pl.ds(C, C), :] = lo
-        return 0
-
-    lax.fori_loop(0, owned * KX, cut, 0)
 
     for b in range(samples):
         arrive(0, b)
         mix(b)
+
+    build_spread(e_unmix, True)
+
+    def turn_over(j, _):
+        for p in range(KX // 2):
+            at = j * KX + p
+            w_t[j * (KX // 2) + p] = jnp.concatenate([w_v[at], w_v[at + KX // 2]], axis=0).T
+        return 0
+
+    lax.fori_loop(0, owned, turn_over, 0)
+
     store[...] = jnp.zeros_like(store)
     for b in range(samples):
         arrive(1, b)
@@ -349,53 +391,44 @@
     n, planes, owned,
     kept_r, modes, grads, lines,
     gm_out, gf_out,
-    t_r, store, lhs, rhs, gm, gf, gm_sem, gf_sem,
+    t_r, store, e_mix, gm, gf, gm_sem, gf_sem,
 ):
     rows = n * 8
     samples = gf.shape[0]
-    low = iota((KX, LANES), 1) < C
-    sign = jnp.where(low, 1.0, -1.0).astype(F32)
-    lhs[...] = jnp.zeros_like(lhs)
-    rhs[...] = jnp.zeros_like(rhs)
-    chunk = KX // 2
-    gm_copies = []
-    for j in range(owned):
-        base = j * KX
-        at = pl.ds(base, KX)
+    sign = jnp.where(iota((KX, LANES), 1) < C, 1.0, -1.0).astype(F32)
+
+    build_spread(e_mix, False)
+
+    def weights(j):
+        at = pl.ds(j * KX, KX)
+        return pltpu.make_async_copy(gm.at[at], gm_out.at[at], gm_sem.at[j])
+
+    def outer(j, _):
+        parts = []
         for b in range(samples):
-            u, g = modes[j, b], grads[j, b]
-            for k, (uu, gg) in enumerate(((u, g), (swap(u), swap(g) * sign))):
-                u_hi = uu.astype(BF16).astype(F32)
-                u_lo = (uu - u_hi).astype(BF16).astype(F32)
-                g_hi = gg.astype(BF16).astype(F32)
-                g_lo = (gg - g_hi).astype(BF16).astype(F32)
-                row = (b * 2 + k) * 3
-                for r, (left, right) in enumerate(((u_hi, g_hi), (u_hi, g_lo), (u_lo, g_hi))):
-                    lhs[at, row + r, :] = left
-                    rhs[at, row + r, :] = right
-    for j in range(owned):
-        base = j * KX
-
-        def body(i, _):
-            for u in range(4):
-                a = base + i * 4 + u
-                got = lax.dot_general(
-                    lhs[a].astype(BF16), rhs[a].astype(BF16), (((0,), (0,)), ((), ())), preferred_element_type=F32
-                )
-                gm[a] = got[:C, :]
-            return 0
-
-        lax.fori_loop(0, KX // 4, body, 0)
-        copy = pltpu.make_async_copy(gm.at[pl.ds(base, KX)], gm_out.at[pl.ds(base, KX)], gm_sem.at[j])
-        copy.start()
-        gm_copies.append(copy)
+            g = grads[j, b]
+            parts.append((turned(modes[j, b]), g, swap(g) * sign))
+        for start in range(0, KX, 4):
+            wide = [dot(lhs, e_mix[:, start * LANES : (start + 4) * LANES]) for lhs, _, _ in parts]
+            for r in range(4):
+                a = start + r
+                got = None
+                for u, (_, g, g_swap) in zip(wide, parts):
+                    u = u[:, r * LANES : (r + 1) * LANES]
+                    term = u[:C] * g[a : a + 1, :] + u[C:] * g_swap[a : a + 1, :]
+                    got = term if got is None else got + term
+                gm[j * KX + a] = got
+        weights(j).start()
+        return 0
+
+    lax.fori_loop(0, owned, outer, 0)
 
     build_rows(kept_r[...], t_r, rows)
     store[...] = jnp.zeros_like(store)
     chunks = gf_sem.shape[1]
     width = CELLS // chunks
     for b in range(samples):
-        first, second = lines_matrix(lines, b, store, n, planes, owned)
+        first = lines_matrix(lines, b, store, n, planes, owned)
 
         def chunk_of(k, b=b):
             at = pl.ds(pl.multiple_of(k * width, width), width)
@@ -403,14 +436,14 @@
 
         def body(k, _):
             at, copy = chunk_of(k)
-            out = dot(first, t_r[:, at]) + dot(second, t_r[pl.ds(0, rows), at])
+            out = dot(first, t_r[:, at])
             gf[b, :, :, at] = out.reshape(planes, C, width)
             copy.start()
             return 0
 
         lax.fori_loop(0, chunks, body, 0)
-    for copy in gm_copies:
-        copy.wait()
+    for j in range(owned):
+        weights(j).wait()
     for b in range(samples):
         def done(k, _, b=b):
             at = pl.ds(pl.multiple_of(k * width, width), width)
@@ -447,13 +480,15 @@
             pltpu.VMEM(field.shape, F32),
             pltpu.VMEM(field.shape, F32),
             pltpu.VMEM((owned * KX, C, LANES), F32),
-            pltpu.VMEM((owned * KX, LANES, LANES), BF16),
-            pltpu.VMEM((2 * rows, CELLS), BF16),
+            pltpu.VMEM((owned * KX // 2, LANES, LANES), F32),
+            pltpu.VMEM((3 * rows, CELLS), BF16),
             pltpu.VMEM((CELLS, 2 * rows), BF16),
             pltpu.VMEM((planes * C, rows), F32),
             pltpu.VMEM((n, 8, planes * C), F32),
-            pltpu.VMEM((owned * KX, 8, LANES), F32),
-            pltpu.VMEM((owned * KX, 8, LANES), F32),
+            pltpu.VMEM((2, 2, planes * C, 256), BF16),
+            pltpu.VMEM((2 * KX, KX * LANES), BF16),
+            pltpu.VMEM((2 * KX, KX * LANES // 2), BF16),
+            pltpu.VMEM((owned * KX, 16, LANES), F32),
             pltpu.VMEM((2, owned, samples, KX, LANES), F32),
             pltpu.VMEM((4, samples) + block, F32),
             pltpu.VMEM((4, samples) + block, F32),
@@ -477,10 +512,9 @@
         in_specs=[vmem, vmem, vmem, vmem],
         out_specs=[hbm, hbm],
         scratch_shapes=[
-            pltpu.VMEM((2 * rows, CELLS), BF16),
+            pltpu.VMEM((3 * rows, CELLS), BF16),
             pltpu.VMEM((n, 8, planes * C), F32),
-            pltpu.VMEM((owned * KX, 16, LANES), F32),
-            pltpu.VMEM((owned * KX, 16, LANES), F32),
+            pltpu.VMEM((2 * KX, KX * LANES), BF16),
             pltpu.VMEM((owned * KX, C, LANES), F32),
             pltpu.VMEM(field.shape, F32),
             pltpu.SemaphoreType.DMA((owned,)),

time: 74.6 us -> 65.3 us (0.88)
  Pallas kernels: 71.4 us -> 62 us
    pallas_call x1, Pallas kernels: 56.5 us -> 50.4 us  [on_device(): pl.pallas_call(functools.partial(main_kernel, n, planes, owned), out_shap...]
    pallas_call x1, Pallas kernels: 14.9 us -> 11.5 us  [on_device(): pl.pallas_call(functools.partial(last_kernel, n, planes, owned), out_shap...]
where the time goes in v1:
time: 65.3 us; the launch traced here: 65.1 us
  Pallas kernels  62 us (95%)
  local copies, waits for them, and re-layouts  2.33 us (4%)
  between operations  0.8 us (1%)
    pallas_call x1, Pallas kernels, on_device(): pl.pallas_call(functools.partial(main_kernel, n, planes, owned), out_shap...  50.4 us
    pallas_call x1, Pallas kernels, on_device(): pl.pallas_call(functools.partial(last_kernel, n, planes, owned), out_shap...  11.5 us

profile of v1, /device:TPU:0, one launch (start us, length us, event | category | flops | bytes accessed | tf_op | source)
XLA Modules:
  0.0 65.1 jit_solution(12365688024470523491)
XLA Ops:
  0.6 0.7 %broadcast_in_dim.19 = s32[16,3]{1,0:T(8,128)S(1)} reshape(s32[48]{0:T(128)} %kept_s.1) | data formatting | bytes 384 | tf_op jit(solution)/shard_map/broadcast_in_dim | solution.py:461
  1.4 0.1 copy.8
  1.5 0.1 copy.10
  1.6 0.1 broadcast_in_dim.21
  1.7 0.6 broadcast_in_dim.23.kept_c
  2.3 0.7 %broadcast_in_dim.22.kept_r = s32[128,128]{1,0:T(8,128)} broadcast(s32[128]{0:T(128)S(1)} %broadcast_in_dim.21), dimensions={0} | broadcast | bytes 66048 | tf_op jit(solution)/shard_map/broadcast_in_dim | solution.py:463
  3.0 50.4 %shard_map.59 = (f32[3,2,32,128]{3,2,1,0:T(8,128)}, f32[3,2,32,128]{3,2,1,0:T(8,128)}, f32[2,16,4,384]{3,2,1,0:T(4,128)}) custom-call(s32[48]{0:T(128)} %kept_s.1, s32[128,128]{1,0:T(8,128)} %broadcast_in_dim.22.kept_r, s32[8,128]{1,0:T(8,128)} %broadcast_in_dim.23.kept_c, f32[2,4,64,4096]{3,2,1,0:T(8,128)} %field.1, f32[2,4,64,4096]{3,2,1,0:T(8,128)} %out_grad.1, ...), custom_call_target="tpu_custom_call" | custom-call | tf_op jit(solution)/shard_map/pallas_call | solution.py:470
  53.4 11.5 %shard_map.60 = (f32[96,64,128]{2,1,0:T(8,128)}, f32[2,4,64,4096]{3,2,1,0:T(8,128)}) custom-call(s32[128,128]{1,0:T(8,128)} %broadcast_in_dim.22.kept_r, f32[3,2,32,128]{3,2,1,0:T(8,128)} %get-tuple-element.7.modes, f32[3,2,32,128]{3,2,1,0:T(8,128)} %get-tuple-element.8.grads, f32[2,16,4,384]{3,2,1,0:T(4,128)} %get-tuple-element.9.lines), custom_call_target="tpu_custom_call" | custom-call | tf_op jit(solution)/shard_map/pallas_call | solution.py:506
  (3 shorter events, 0.0 us)
